TPU v7x, 32 devices: a whole 2x2x4 slice. The times are simulated.
32 devices in a mesh: group: 2 (over x), row: 16 (over z, y, core).
Axes of the slice: x: 2, y: 2, z: 4, core: 2. Of those that a mesh axis runs over, the one named last changes fastest.
Arguments:
- features: float32 [8192, 128], P(('group', 'row')), parts along dimension 0, may hold values from -90 to 90
- w_left: float32 [128, 512], replicated, may hold values from -0.5 to 0.5
- w_right: float32 [128, 512], replicated, may hold values from -0.5 to 0.5
- attention: float32 [8, 64], replicated, may hold values from -0.75 to 0.75
- requests: int32 [32, 16], P(('group', 'row')), parts along dimension 0, may hold values from -1 to 7, as said below
- src_slot: int32 [8192, 8], P(('group', 'row')), parts along dimension 0, may hold values from 0 to 511, as said below
- edge_mask: int32 [8192, 8], P(('group', 'row')), parts along dimension 0, may hold values from 0 to 1, as said below
- g_out: float32 [8192, 512], P(('group', 'row')), parts along dimension 0, may hold values from -6 to 6
Outputs:
- out: float32 [8192, 512], P(('group', 'row')), parts along dimension 0
- feature_gradient: float32 [8192, 128], P(('group', 'row')), parts along dimension 0
- grad_left: float32 [256, 512], P('group'), parts along dimension 0
- grad_right: float32 [256, 512], P('group'), parts along dimension 0
- grad_att: float32 [16, 64], P('group'), parts along dimension 0
There are 2 independent parts, one for each index of `group`. A program takes and returns all parts, laid end to end along the dimension named above; an argument that names none is the same for every part. Nothing has to cross between parts.
Inputs may be any that keep to these rules, and one draw needn't show every extreme that they name: `requests`: each device reads at most one tile of each device. `src_slot`: every entry names a slot p * 32 + r whose request requests[d, p] on the destination's device d is not -1. `edge_mask`: the first slot of every row is live.
All inputs are finite; a program needn't handle non-finite values.
Results may differ from a plain program's by a relative error of at most 0.007.
Values sent between devices are 32-bit elements; how exact they have to be, the bound alone decides.
A program may use at most 128 MiB of HBM per device.

v0:
```python
import jax
import jax.numpy as jnp
from jax import lax
from jax.sharding import PartitionSpec as P

FI = 128
HEADS = 8
HD = 64
TILE = 32
DEG = 8


HIGH_PRECISION = lax.Precision.HIGHEST


def attend(left_e, right_rows, attention, live, g_rows):
    z = left_e + right_rows[:, None]
    slope = jnp.where(z > 0, 1.0, 0.2).astype(z.dtype)
    u = z * slope
    score = jnp.einsum("behc,hc->beh", u, attention, precision=HIGH_PRECISION)
    alive = live[:, :, None] > 0
    score = jnp.where(alive, score, -1e30)
    top = jnp.max(score, axis=1, keepdims=True)
    weights = jnp.exp(score - top) * alive.astype(score.dtype)
    prob = weights / jnp.sum(weights, axis=1, keepdims=True)
    out_rows = jnp.einsum("beh,behc->bhc", prob, left_e, precision=HIGH_PRECISION)
    dprob = jnp.einsum("bhc,behc->beh", g_rows, left_e, precision=HIGH_PRECISION)
    dscore = prob * (dprob - jnp.sum(prob * dprob, axis=1, keepdims=True))
    inner = dscore[..., None] * attention[None, None] * slope
    d_left = prob[..., None] * g_rows[:, None] + inner
    right_gradient = jnp.sum(inner, axis=1)
    d_att = jnp.einsum("beh,behc->hc", dscore, u, precision=HIGH_PRECISION)
    return (out_rows, d_left, right_gradient, d_att)


def matmul(first, second):
    return jnp.dot(first, second, precision=HIGH_PRECISION, preferred_element_type=jnp.float32)


def transposed(first, second):
    return lax.dot_general(
        first,
        second,
        (((0,), (0,)), ((), ())),
        precision=HIGH_PRECISION,
        preferred_element_type=jnp.float32,
    )


def on_device(features, w_left, w_right, attention, requests, src_slot, edge_mask, g_out):
    peers = lax.axis_size("row")
    rows = features.shape[0]
    width = HEADS * HD
    tiles_dev = rows // TILE
    asked = lax.all_to_all(requests, "row", split_axis=1, concat_axis=1, tiled=True)
    selector_matrix = (asked[0][:, None] == jnp.arange(tiles_dev, dtype=jnp.int32)[None, :]).astype(
        jnp.float32
    )
    local_tile_rows = features.reshape(tiles_dev, TILE, FI)
    outbound_messages = jnp.einsum(
        "dl,lxm->dxm", selector_matrix, local_tile_rows, precision=HIGH_PRECISION
    )
    fetched = lax.all_to_all(outbound_messages, "row", split_axis=0, concat_axis=0, tiled=True)
    fetched_rows = fetched.reshape(peers * TILE, FI)
    left = matmul(fetched_rows, w_left)
    right = matmul(features, w_right)
    block = 256
    count = rows // block

    def step(carry, blocks):
        d_left_buf, d_att = carry
        src_b, live_batch_mask, right_b, g_b = blocks
        left_e = left[src_b].reshape(block, DEG, HEADS, HD)
        out_b, d_l, d_r, d_a = attend(
            left_e,
            right_b.reshape(block, HEADS, HD),
            attention,
            live_batch_mask,
            g_b.reshape(block, HEADS, HD),
        )
        d_left_buf = d_left_buf.at[src_b.reshape(-1)].add(d_l.reshape(-1, width))
        return ((d_left_buf, d_att + d_a), (out_b.reshape(block, width), d_r.reshape(block, width)))

    blocks = (
        src_slot.reshape(count, block, DEG),
        edge_mask.reshape(count, block, DEG),
        right.reshape(count, block, width),
        g_out.reshape(count, block, width),
    )
    start = (jnp.zeros((peers * TILE, width), jnp.float32), jnp.zeros((HEADS, HD), jnp.float32))
    (d_left_buf, d_att), (out_blocks, d_right_blocks) = lax.scan(step, start, blocks)
    out = out_blocks.reshape(rows, width)
    right_gradient = d_right_blocks.reshape(rows, width)
    returned = lax.all_to_all(
        d_left_buf.reshape(peers, TILE, width), "row", split_axis=0, concat_axis=0, tiled=True
    )
    local_left_part = jnp.einsum(
        "qt,qrh->trh", selector_matrix, returned, precision=HIGH_PRECISION
    ).reshape(rows, width)
    feature_gradient = matmul(local_left_part, w_left.T) + matmul(right_gradient, w_right.T)
    left_part = transposed(features, local_left_part)
    right_part = transposed(features, right_gradient)
    grad_left, grad_right, grad_att = lax.psum((left_part, right_part, d_att), "row")
    return (out, feature_gradient, grad_left, grad_right, grad_att)


def solution(mesh):
    in_specs = (
        P(("group", "row"), None),
        P(),
        P(),
        P(),
        P(("group", "row"), None),
        P(("group", "row"), None),
        P(("group", "row"), None),
        P(("group", "row"), None),
    )
    out_specs = (
        P(("group", "row"), None),
        P(("group", "row"), None),
        P("group", None),
        P("group", None),
        P("group", None),
    )
    return jax.shard_map(
        on_device, mesh=mesh, in_specs=in_specs, out_specs=out_specs, check_vma=False
    )
```

profile of v0, /device:TPU:1, one launch (start us, length us, event | category | flops | bytes accessed | tf_op | source)
XLA Modules:
  0.0 287.5 jit_solution(1331119682521105389)
XLA Ops:
  7.2 1.4 copy.51
  8.6 7.3 %all-to-all-start = ((s32[1,16,1]{2,0,1:T(1,128)}), s32[1,16,1]{2,0,1:T(1,128)S(1)}, u32[]{:S(2)}, u32[]{:S(2)}) async-start(s32[1,16,1]{2,0,1:T(1,128)} %copy.51), calls=%async_computation | async-start | bytes 16384 | tf_op jit(solution)/shard_map/all_to_all | solution.py:55
  17.3 1.6 fusion.40
  19.2 2.4 all-to-all-done
  24.0 4.6 %all-to-all-start.1 = ((f32[16,32,128]{2,1,0:T(8,128)}), f32[16,32,128]{2,1,0:T(8,128)}, u32[]{:S(2)}, u32[]{:S(2)}) async-start(f32[16,32,128]{2,1,0:T(8,128)} %copy.53), calls=%async_computation.1 | async-start | bytes 524288 | tf_op jit(solution)/shard_map/all_to_all | solution.py:63
  33.9 3.8 %add.60 = f32[256,8,8,64]{3,2,1,0:T(8,128)} broadcast(f32[256,8,64]{2,1,0:T(8,128)S(1)} %copy.56), dimensions={0,2,3} | broadcast | bytes 4718592 | tf_op jit(solution)/shard_map/while/body/eval_jaxpr/add | solution.py:17
  37.7 7.5 %add.63 = f32[2048,512]{1,0:T(8,128)} reshape(f32[256,8,8,64]{3,2,1,0:T(8,128)} %add.60) | data formatting | bytes 8388608 | tf_op jit(solution)/shard_map/while/body/eval_jaxpr/add | solution.py:17
  45.8 1.9 fusion.39
  47.7 8.9 %gather_fusion = f32[2048,512]{1,0:T(8,128)} fusion(f32[512,512]{1,0:T(8,128)S(1)} %fusion.39, s32[2048]{0:T(1024)S(1)} %broadcast_clamp_fusion), kind=kCustom, calls=%fused_computation | custom fusion | bytes 8396800 | tf_op jit(solution)/shard_map/while/body/eval_jaxpr/gather | solution.py:73
  56.7 7.0 %reshape.143 = f32[256,8,8,64]{3,2,1,0:T(8,128)} reshape(f32[2048,512]{1,0:T(8,128)} %gather_fusion) | data formatting | bytes 8388608 | tf_op jit(solution)/shard_map/while/body/eval_jaxpr/reshape | solution.py:73
  63.7 6.8 %multiply_reduce_fusion.3 = f32[8,256,8]{0,2,1:T(8,128)} fusion(f32[256,8,8,64]{3,2,1,0:T(8,128)} %reshape.143, f32[8,64]{1,0:T(8,128)S(1)} %copy-done.7, f32[256,8,64]{2,1,0:T(8,128)S(1)} %copy.56), kind=kLoop, calls=%fused_computation.9 | loop fusion | flops 6275072 | bytes 4786176 | tf_op jit(solution)/shard_map/while/body/eval_jaxpr/behc,hc->beh/dot_general | solution.py:20
  70.5 3.4 %multiply_reduce_fusion.1 = f32[256,8,8]{1,2,0:T(8,128)} fusion(f32[256,8,8,64]{3,2,1,0:T(8,128)S(1)} %copy-done.1, f32[256,8,64]{2,1,0:T(8,128)S(1)} %copy.60), kind=kLoop, calls=%fused_computation.7 | loop fusion | flops 2080768 | bytes 4784128 | tf_op jit(solution)/shard_map/while/body/eval_jaxpr/bhc,behc->beh/dot_general | solution.py:27
  73.9 2.1 fusion.23
  76.0 4.6 %broadcast_multiply_fusion = f32[256,8,8,64]{3,2,1,0:T(8,128)} fusion(f32[256,8,64]{2,1,0:T(8,128)S(1)} %copy-done.3, f32[256,8,8]{2,1,0:T(8,128)S(1)} %fusion.23), kind=kLoop, calls=%fused_computation.16 | loop fusion | flops 1048576 | bytes 4784128 | tf_op jit(solution)/shard_map/while/body/eval_jaxpr/mul | solution.py:30
  80.6 5.2 %fusion.15 = f32[256,8,8]{2,1,0:T(8,128)S(1)} fusion(f32[256,8,8]{2,1,0:T(8,128)S(1)} %fusion.23, f32[256,8,8]{1,2,0:T(8,128)S(1)} %copy-done.4), kind=kOutput, calls=%fused_computation.30 | output fusion | flops 51207 | bytes 196608 | tf_op jit(solution)/shard_map/while/body/eval_jaxpr/sub | solution.py:28
  85.8 7.5 %mul.101 = f32[2048,512]{1,0:T(8,128)} reshape(f32[256,8,8,64]{3,2,1,0:T(8,128)} %broadcast_multiply_fusion) | data formatting | bytes 8388608 | tf_op jit(solution)/shard_map/while/body/eval_jaxpr/mul | solution.py:30
  93.3 4.6 %mul.104 = f32[256,8,8,64]{3,2,1,0:T(8,128)} broadcast(f32[256,8,8]{2,1,0:T(8,128)S(1)} %fusion.15), dimensions={0,1,2} | broadcast | bytes 4259840 | tf_op jit(solution)/shard_map/while/body/eval_jaxpr/mul | solution.py:29
  97.9 7.5 %mul.105 = f32[2048,512]{1,0:T(8,128)} reshape(f32[256,8,8,64]{3,2,1,0:T(8,128)} %mul.104) | data formatting | bytes 8388608 | tf_op jit(solution)/shard_map/while/body/eval_jaxpr/mul | solution.py:29
  105.4 16.0 %scatter_custom_fusion = f32[512,512]{1,0:T(8,128)} fusion(s32[2048]{0:T(1024)} %bitcast.71, f32[2048,512]{1,0:T(8,128)} %mul.101, f32[2048,512]{1,0:T(8,128)} %mul.105, f32[2048,512]{1,0:T(8,128)} %gather_fusion, f32[2048,512]{1,0:T(8,128)} %add.63, f32[]{:T(128)} %constant.20.clone.1, f32[]{:T(128)} %constant.18.clone.1, f32[]{:T(128)} %constant.16.clone.1, ...), kind=kCustom, calls=%fused_computation.10 | custom fusion | flops 7340032 | bytes 17829888 | tf_op jit(solution)/shard_map/while/body/eval_jaxpr/scatter-add | solution.py:81
  121.4 6.1 %all-to-all-start.2 = ((f32[16,32,512]{2,1,0:T(8,128)}), f32[16,32,512]{2,1,0:T(8,128)}, u32[]{:S(2)}, u32[]{:S(2)}) async-start(f32[16,32,512]{2,1,0:T(8,128)} %bitcast.66), calls=%async_computation.2 | async-start | bytes 2097152 | tf_op jit(solution)/shard_map/all_to_all | solution.py:94
  127.5 6.3 %multiply_reduce_fusion.2 = f32[256,8,64]{2,1,0:T(8,128)} fusion(f32[256,8,8,64]{3,2,1,0:T(8,128)} %reshape.143, f32[256,8,8]{1,2,0:T(8,128)S(1)} %bitcast.61), kind=kLoop, calls=%fused_computation.8 | loop fusion | flops 1966080 | bytes 4784128
  133.9 1.5 copy.81
  136.4 6.3 %fusion.1 = f32[256,8,64]{2,1,0:T(8,128)} fusion(f32[256,8,8,64]{3,2,1,0:T(8,128)} %reshape.143, f32[8,64]{1,0:T(8,128)S(1)} %copy-done.7, f32[256,8,8]{2,1,0:T(8,128)S(1)} %fusion.15, f32[256,8,64]{2,1,0:T(8,128)S(1)} %copy.56), kind=kLoop, calls=%fused_computation.5 | loop fusion | flops 6160384 | bytes 5310464 | tf_op jit(solution)/shard_map/while/body/eval_jaxpr/reduce_sum | solution.py:31
  142.7 1.6 copy.63
  144.3 5.2 %multiply_reduce_fusion = f32[8,64]{1,0:T(8,128)S(1)} fusion(f32[256,8,8,64]{3,2,1,0:T(8,128)} %reshape.143, f32[8,256,8]{0,2,1:T(8,128)S(1)} %bitcast.60, f32[256,8,64]{2,1,0:T(8,128)S(1)} %copy.56), kind=kLoop, calls=%fused_computation.6 | loop fusion | flops 6290944 | bytes 4786176 | tf_op jit(solution)/shard_map/while/body/eval_jaxpr/beh,behc->hc/dot_general | solution.py:32
  149.5 29.8 %psum.23 = f32[8,64]{1,0:T(8,128)} all-reduce(f32[8,64]{1,0:T(8,128)S(1)} %multiply_reduce_fusion), channel_id=1, replica_groups=mesh['group'=2,'row'=16] {'row'}, use_global_device_ids=true, to_apply=%region_7.8 | all-reduce | flops 512 | bytes 4096 | tf_op jit(solution)/shard_map/psum | solution.py:103
  180.7 2.2 fusion.17
  183.2 1.7 convolution_bitcast_fusion.1
  185.5 1.7 convolution_add_fusion
  187.2 89.9 %all-reduce.3.cloned.1.call-done = (f32[128,512]{0,1:T(8,128)}, f32[128,512]{0,1:T(8,128)}) async-done(((f32[128,512]{0,1:T(8,128)}, f32[128,512]{0,1:T(8,128)}), (f32[128,512]{0,1:T(8,128)}, f32[128,512]{0,1:T(8,128)})) %all-reduce.3.cloned.1.call-update) | async-done | bytes 524304 | tf_op jit(solution)/shard_map/psum | solution.py:103
  277.1 1.8 copy.65
  278.9 1.8 copy.66
  (47 shorter events, 13.1 us)
Async XLA Ops:
  7.2 38.7 %copy-start = (f32[128,512]{1,0:T(8,128)S(1)}, f32[128,512]{1,0:T(8,128)}, u32[]{:S(2)}) copy-start(f32[128,512]{1,0:T(8,128)} %param.9) | copy-start | bytes 786436
  8.6 13.1 %all-to-all-start = ((s32[1,16,1]{2,0,1:T(1,128)}), s32[1,16,1]{2,0,1:T(1,128)S(1)}, u32[]{:S(2)}, u32[]{:S(2)}) async-start(s32[1,16,1]{2,0,1:T(1,128)} %copy.51), calls=%async_computation | async-start | bytes 16384 | tf_op jit(solution)/shard_map/all_to_all | solution.py:55
  22.0 6.7 %copy-start.9 = (s32[16]{0:T(128)}, s32[16]{0:T(128)S(1)}, u32[]{:S(2)}) copy-start(s32[16]{0:T(128)S(1)} %reduce.8) | copy-start | bytes 196
  24.0 21.8 %all-to-all-start.1 = ((f32[16,32,128]{2,1,0:T(8,128)}), f32[16,32,128]{2,1,0:T(8,128)}, u32[]{:S(2)}, u32[]{:S(2)}) async-start(f32[16,32,128]{2,1,0:T(8,128)} %copy.53), calls=%async_computation.1 | async-start | bytes 524288 | tf_op jit(solution)/shard_map/all_to_all | solution.py:63
  33.5 37.0 %copy-start.2 = (f32[256,8,64]{2,1,0:T(8,128)}, f32[256,8,64]{2,1,0:T(8,128)S(1)}, u32[]{:S(2)}) copy-start(f32[256,8,64]{2,1,0:T(8,128)S(1)} %copy.60) | copy-start | bytes 1572868
  56.7 7.0 %copy-start.7 = (f32[8,64]{1,0:T(8,128)S(1)}, f32[8,64]{1,0:T(8,128)}, u32[]{:S(2)}) copy-start(f32[8,64]{1,0:T(8,128)} %param.11) | copy-start | bytes 6148
  63.7 6.8 %copy-start.1 = (f32[256,8,8,64]{3,2,1,0:T(8,128)S(1)}, f32[256,8,8,64]{3,2,1,0:T(8,128)}, u32[]{:S(2)}) copy-start(f32[256,8,8,64]{3,2,1,0:T(8,128)} %reshape.143) | copy-start | bytes 12582916
  73.9 2.1 copy-start.3
  76.0 4.6 %copy-start.4 = (f32[256,8,8]{1,2,0:T(8,128)S(1)}, f32[256,8,8]{1,2,0:T(8,128)}, u32[]{:S(2)}) copy-start(f32[256,8,8]{1,2,0:T(8,128)} %multiply_reduce_fusion.1) | copy-start | bytes 196612
  97.9 7.5 %copy-start.8 = (f32[512]{0:T(512)S(1)}, f32[512]{0:T(512)}, u32[]{:S(2)}) copy-start(f32[512]{0:T(512)} %mul.106) | copy-start | bytes 6148
  121.4 59.3 %all-to-all-start.2 = ((f32[16,32,512]{2,1,0:T(8,128)}), f32[16,32,512]{2,1,0:T(8,128)}, u32[]{:S(2)}, u32[]{:S(2)}) async-start(f32[16,32,512]{2,1,0:T(8,128)} %bitcast.66), calls=%async_computation.2 | async-start | bytes 2097152 | tf_op jit(solution)/shard_map/all_to_all | solution.py:94
  127.5 149.6 %all-reduce.3.cloned.1.call-start = ((), (), s32[]{:S(2)}) async-start(), calls=%async_computation.3 | async-start | bytes 1048576 | tf_op jit(solution)/shard_map/psum | solution.py:103
  142.7 36.7 %copy-start.5 = (f32[256,128]{1,0:T(8,128)S(1)}, f32[256,128]{1,0:T(8,128)}, u32[]{:S(2)}) copy-start(f32[256,128]{1,0:T(8,128)} %param.8) | copy-start | bytes 393220
  142.7 38.0 %copy-start.10 = (s32[16]{0:T(128)S(1)}, s32[16]{0:T(128)}, u32[]{:S(2)}) copy-start(s32[16]{0:T(128)} %copy-done.9) | copy-start | bytes 196
  144.3 41.3 %copy-start.6 = (f32[128,512]{1,0:T(8,128)S(1)}, f32[128,512]{1,0:T(8,128)}, u32[]{:S(2)}) copy-start(f32[128,512]{1,0:T(8,128)} %param.10) | copy-start | bytes 786436
Sparse Core Ops, SparseCore 0:
  185.1 91.9 all-reduce.2
where the time goes:
time: 289 us; the launch traced here: 287 us
  waiting for transfers between devices  92.3 us (32%)
  local copies, waits for them, and re-layouts  62.4 us (22%)
  other arithmetic  58.3 us (20%)
  blocking collectives  29.8 us (10%)
  starting transfers between devices  18.1 us (6%)
  between operations  14.3 us (5%)
  matrix products  12.2 us (4%)
    psum x1, waiting for transfers between devices, on_device(): lax.psum((left_part, right_part, d_att), 'row')  89.9 us
    psum x1, blocking collectives, on_device(): lax.psum((left_part, right_part, d_att), 'row')  29.8 us
    scatter-add x1, other arithmetic, step(): d_left_buf = d_left_buf.at[src_b.reshape(-1)].add(d_l.reshape(-1, width))  16 us
    mul x3, local copies, waits for them, and re-layouts, attend(): inner = dscore[..., None] * attention[None, None] * slope  13.4 us
    add x3, local copies, waits for them, and re-layouts, attend(): z = left_e + right_rows[:, None]  11.7 us
    gather x1, local copies, waits for them, and re-layouts, step(): left_e = left[src_b].reshape(block, DEG, HEADS, HD)  8.91 us
    mul x2, local copies, waits for them, and re-layouts, attend(): d_left = prob[..., None] * g_rows[:, None] + inner  7.9 us
    all_to_all x1, starting transfers between devices, on_device(): lax.all_to_all(requests, 'row', split_axis=1, concat_axis=1, tiled=True)  7.35 us
  transfers between devices with their start and end apart: 4, of which 2 were waited for; matrix products, arithmetic and copies ran while one was open for 16% of the time, Pallas kernels for 0%

commit v1 on v0

v1 whole, which is shorter than its diff:
```python
import functools

import jax
import jax.numpy as jnp
from jax import lax
from jax.experimental import pallas as pl
from jax.experimental.pallas import tpu as pltpu
from jax.sharding import PartitionSpec as P

FI = 128
HEADS = 8
HD = 64
TILE = 32
DEG = 8
WIDTH = HEADS * HD
LANES = 128
CHUNK = 512

HIGHEST = lax.Precision.HIGHEST
MESH = pl.DeviceIdType.MESH
BF16 = jnp.bfloat16
F32 = jnp.float32


def dot(a, b, dims=((1,), (0,)), precision=None):
    return lax.dot_general(a, b, (dims, ((), ())), precision=precision, preferred_element_type=F32)


def split(x):
    hi = x.astype(BF16)
    return hi, (x - hi.astype(F32)).astype(BF16)


def split3(x):
    hi = x.astype(BF16)
    rest = x - hi.astype(F32)
    mid = rest.astype(BF16)
    return hi, mid, (rest - mid.astype(F32)).astype(BF16)


def greet(n, me, barrier):
    @pl.loop(1, n)
    def _(k):
        pl.semaphore_signal(barrier, inc=1, device_id={"row": lax.rem(me + k, n)}, device_id_type=MESH)

    pl.semaphore_wait(barrier, n - 1)


def fetch_kernel(n, req_ref, feat_ref, fetched_ref, asked_ref, ask_out, tile_out, ask_in, tile_in, sems):
    me = lax.axis_index("row")
    tiles = feat_ref.shape[0] // TILE
    barrier = pltpu.get_barrier_semaphore()

    def ask(k):
        peer = lax.rem(me + k, n)
        return pltpu.make_async_remote_copy(
            src_ref=ask_out.at[peer], dst_ref=ask_in.at[me], send_sem=sems.at[0, k], recv_sem=sems.at[1, k],
            device_id={"row": peer}, device_id_type=MESH)

    def give(k):
        peer = lax.rem(me + k, n)
        return pltpu.make_async_remote_copy(
            src_ref=tile_out.at[peer], dst_ref=tile_in.at[me], send_sem=sems.at[2, k], recv_sem=sems.at[3, k],
            device_id={"row": peer}, device_id_type=MESH)

    for p in range(n):
        ask_out[p] = jnp.full((8, LANES), req_ref[0, p], jnp.int32)
    greet(n, me, barrier)

    @pl.loop(1, n)
    def _(k):
        ask(k).start()

    feats = [feat_ref[t * TILE:(t + 1) * TILE].reshape(TILE // 8, 8, FI) for t in range(tiles)]

    def chosen(want):
        total = jnp.zeros((TILE // 8, 8, FI), F32)
        for t in range(tiles):
            total = total + jnp.where((want == t)[None], feats[t], 0.0)
        return total.reshape(TILE, FI)

    tile_in[me] = chosen(ask_out[me])
    ask_in[me] = ask_out[me]

    @pl.loop(1, n)
    def _(j):
        k = n - j
        ask(k).wait_recv()
        peer = lax.rem(me + j, n)
        tile_out[peer] = chosen(ask_in[peer])
        give(j).start()

    @pl.loop(1, n)
    def _(k):
        give(k).wait_recv()
        ask(k).wait_send()
        give(k).wait_send()

    fetched_ref[...] = tile_in[...].reshape(n * TILE, FI)
    asked_ref[...] = ask_in[...]


def local_kernel(n, fetched_ref, feat_ref, wl_ref, wr_ref, att_ref, slot_ref, mask_ref, g_ref,
                 out_ref, ret_ref, fg_ref, msg_ref, hi_ref, mid_ref, lo_ref, le_ref, dhi_ref, dlo_ref, wg_ref):
    rows = feat_ref.shape[0]
    slots_all = fetched_ref.shape[0]
    chunks = slots_all // CHUNK
    left = dot(fetched_ref[...], wl_ref[...], precision=HIGHEST) if chunks == 1 else None
    if chunks == 1:
        hi_ref[...], mid_ref[...], lo_ref[...] = split3(left)
    else:
        @pl.loop(0, chunks)
        def _(c):
            at = pl.ds(pl.multiple_of(c * CHUNK, CHUNK), CHUNK)
            hi_ref[at], mid_ref[at], lo_ref[at] = split3(dot(fetched_ref[at], wl_ref[...], precision=HIGHEST))
    right = dot(feat_ref[...], wr_ref[...], precision=HIGHEST)
    att = att_ref[...]
    g = g_ref[...]
    slot = slot_ref[...]

    row_head = lax.broadcasted_iota(jnp.int32, (WIDTH, LANES), 0) // HD
    col = lax.broadcasted_iota(jnp.int32, (WIDTH, LANES), 1)
    row_match = row_head == (col & 7)
    col_edge = (col >> 3) & 7
    score = jnp.zeros((rows, LANES), F32)
    dp = jnp.zeros((rows, LANES), F32)
    slot_lane = lax.broadcasted_iota(jnp.int32, (rows, CHUNK), 1)
    for e in range(DEG):
        here = slot[:, e:e + 1]
        if chunks == 1:
            pick = (slot_lane == here).astype(F32).astype(BF16)
            left_e = dot(pick, hi_ref[...]) + (dot(pick, mid_ref[...]) + dot(pick, lo_ref[...]))
            le_ref[e] = left_e
        else:
            le_ref[e] = jnp.zeros((rows, WIDTH), F32)

            @pl.loop(0, chunks)
            def _(c):
                at = pl.ds(pl.multiple_of(c * CHUNK, CHUNK), CHUNK)
                pick = (slot_lane + c * CHUNK == here).astype(F32).astype(BF16)
                le_ref[e] += dot(pick, hi_ref[at]) + (dot(pick, mid_ref[at]) + dot(pick, lo_ref[at]))

            left_e = le_ref[e]
        z = left_e + right
        group = (row_match & (col_edge == e)).astype(F32).astype(BF16)
        v_hi, v_lo = split(jnp.maximum(z, 0.2 * z) * att)
        score = score + (dot(v_hi, group) + dot(v_lo, group))
        p_hi, p_lo = split(g * left_e)
        dp = dp + (dot(p_hi, group) + dot(p_lo, group))

    spread = (lax.broadcasted_iota(jnp.int32, (DEG, LANES), 0)
              == ((lax.broadcasted_iota(jnp.int32, (DEG, LANES), 1) >> 3) & 7)).astype(F32)
    alive = dot((mask_ref[...] > 0).astype(F32), spread) > 0.5

    def over_edges(x, op):
        for shift in (8, 16, 32):
            x = op(x, pltpu.roll(x, shift, 1))
        return x

    score = jnp.where(alive, score, -1e30)
    top = over_edges(score, jnp.maximum)
    weights = jnp.where(alive, jnp.exp(score - top), 0.0)
    prob = weights / over_edges(weights, jnp.add)
    ds = prob * (dp - over_edges(prob * dp, jnp.add))
    first_half = lax.broadcasted_iota(jnp.int32, (rows, LANES), 1) < LANES // 2

    def halves(x):
        hi = x.astype(BF16).astype(F32)
        return jnp.where(first_half, hi, x - hi).astype(BF16)

    prob_hl = halves(prob)
    ds_hl = halves(ds)

    krow = lax.broadcasted_iota(jnp.int32, (LANES, WIDTH), 0)
    kmatch = (krow & 7) == lax.broadcasted_iota(jnp.int32, (LANES, WIDTH), 1) // HD
    kedge = (krow >> 3) & 7
    out = jnp.zeros((rows, WIDTH), F32)
    d_right = jnp.zeros((rows, WIDTH), F32)
    d_att = jnp.zeros((8, WIDTH), F32)
    for e in range(DEG):
        widen = (kmatch & (kedge == e)).astype(F32).astype(BF16)
        prob_w = dot(prob_hl, widen)
        ds_w = dot(ds_hl, widen)
        left_e = le_ref[e]
        z = left_e + right
        slope = jnp.where(z > 0, 1.0, 0.2)
        out = out + prob_w * left_e
        t = ds_w * slope
        inner = t * att
        d_right = d_right + inner
        d_att = d_att + jnp.sum((t * z).reshape(rows // 8, 8, WIDTH), axis=0)
        dhi_ref[e * rows:(e + 1) * rows], dlo_ref[e * rows:(e + 1) * rows] = split(prob_w * g + inner)
    out_ref[...] = out

    slot_t = slot.T
    slot_row = lax.broadcasted_iota(jnp.int32, (CHUNK, rows), 0)

    def scatter(c):
        total = jnp.zeros((CHUNK, WIDTH), F32)
        for e in range(DEG):
            put = (slot_row + c * CHUNK == slot_t[e:e + 1]).astype(F32).astype(BF16)
            total = total + (dot(put, dhi_ref[e * rows:(e + 1) * rows]) + dot(put, dlo_ref[e * rows:(e + 1) * rows]))
        return total

    if chunks == 1:
        d_left = scatter(0)
        ret_ref[...] = dot(d_left, wl_ref[...], ((1,), (1,)), precision=HIGHEST)
        wg_ref[0:FI] = dot(fetched_ref[...].T, d_left, precision=HIGHEST)
    else:
        wg_ref[0:FI] = jnp.zeros((FI, WIDTH), F32)

        @pl.loop(0, chunks)
        def _(c):
            at = pl.ds(pl.multiple_of(c * CHUNK, CHUNK), CHUNK)
            d_left = scatter(c)
            ret_ref[at] = dot(d_left, wl_ref[...], ((1,), (1,)), precision=HIGHEST)
            wg_ref[0:FI] += dot(fetched_ref[at].T, d_left, precision=HIGHEST)
    fg_ref[...] = dot(d_right, wr_ref[...], ((1,), (1,)), precision=HIGHEST)
    wg_ref[FI:2 * FI] = dot(feat_ref[...].T, d_right, precision=HIGHEST)

    unit, per = units(n)
    for u in range(n * per):
        rb, lb = u // 4, u % 4
        msg_ref[u // per, (u % per) * unit:(u % per + 1) * unit] = (
            wg_ref[rb * unit:(rb + 1) * unit, lb * LANES:(lb + 1) * LANES])
    att_row = jnp.sum(d_att, axis=0, keepdims=True)
    tail = jnp.concatenate([att_row[:, b * LANES:(b + 1) * LANES] for b in range(4)] + [jnp.zeros((4, LANES), F32)], axis=0)
    for p in range(n):
        msg_ref[p, per * unit:] = tail


def units(n):
    unit = max(8, 2 * FI // n)
    return unit, (2 * FI // unit) * 4 // n


def return_kernel(n, ret_ref, fg_ref, msg_ref, asked_ref, fgo_ref, gl_ref, gr_ref, ga_ref,
                  ret_in, msg_in, sum_out, sum_in, sems):
    me = lax.axis_index("row")
    unit, per = units(n)
    body = unit * per
    barrier = pltpu.get_barrier_semaphore()

    def remote(src, dst, lane, k):
        return pltpu.make_async_remote_copy(
            src_ref=src, dst_ref=dst, send_sem=sems.at[2 * lane, k], recv_sem=sems.at[2 * lane + 1, k],
            device_id={"row": lax.rem(me + k, n)}, device_id_type=MESH)

    def send_msg(k):
        return remote(msg_ref.at[lax.rem(me + k, n)], msg_in.at[me], 0, k)

    def send_ret(k):
        return remote(ret_ref.at[lax.rem(me + k, n)], ret_in.at[me], 1, k)

    def send_sum(k):
        return remote(sum_out, sum_in.at[me], 2, k)

    greet(n, me, barrier)

    @pl.loop(1, n)
    def _(k):
        send_msg(k).start()

    @pl.loop(1, n)
    def _(k):
        send_ret(k).start()

    msg_in[me] = msg_ref[me]
    ret_in[me] = ret_ref[me]

    @pl.loop(1, n)
    def _(k):
        send_msg(k).wait_recv()

    total = lax.fori_loop(1, n, lambda p, acc: acc + msg_in[p], msg_in[0])
    sum_out[...] = total[:body]

    @pl.loop(1, n)
    def _(k):
        send_sum(k).start()

    sum_in[me] = total[:body]
    for b in range(4):
        ga_ref[2 * b:2 * b + 1] = total[body + b:body + b + 1, :HD]
        ga_ref[2 * b + 1:2 * b + 2] = total[body + b:body + b + 1, HD:]

    @pl.loop(1, n)
    def _(k):
        send_ret(k).wait_recv()

    tiles = fg_ref.shape[0] // TILE

    def collect(q, acc):
        want = asked_ref[q]
        back = ret_in[q].reshape(TILE // 8, 8, FI)
        return tuple(acc[t] + jnp.where((want == t)[None], back, 0.0) for t in range(tiles))

    start = tuple(fg_ref[t * TILE:(t + 1) * TILE].reshape(TILE // 8, 8, FI) for t in range(tiles))
    done = lax.fori_loop(0, n, collect, start)
    for t in range(tiles):
        fgo_ref[t * TILE:(t + 1) * TILE] = done[t].reshape(TILE, FI)

    @pl.loop(1, n)
    def _(k):
        send_sum(k).wait_recv()

    for u in range(n * per):
        rb, lb = u // 4, u % 4
        ref, base = (gl_ref, 0) if rb * unit < FI else (gr_ref, FI)
        ref[rb * unit - base:(rb + 1) * unit - base, lb * LANES:(lb + 1) * LANES] = (
            sum_in[u // per, (u % per) * unit:(u % per + 1) * unit])

    @pl.loop(1, n)
    def _(k):
        send_msg(k).wait_send()
        send_ret(k).wait_send()
        send_sum(k).wait_send()


def on_device(features, w_left, w_right, attention, requests, src_slot, edge_mask, g_out):
    n = lax.axis_size("row")
    rows = features.shape[0]
    vmem = pl.BlockSpec(memory_space=pltpu.VMEM)
    smem = pl.BlockSpec(memory_space=pltpu.SMEM)
    limit = 56 * 2**20 if n > 16 else 40 * 2**20

    def shape(*dims, kind=F32):
        return jax.ShapeDtypeStruct(dims, kind)

    fetched, asked = pl.pallas_call(
        functools.partial(fetch_kernel, n),
        out_shape=(shape(n * TILE, FI), shape(n, 8, LANES, kind=jnp.int32)),
        in_specs=[smem, vmem],
        out_specs=(vmem, vmem),
        scratch_shapes=[
            pltpu.VMEM((n, 8, LANES), jnp.int32),
            pltpu.VMEM((n, TILE, FI), F32),
            pltpu.VMEM((n, 8, LANES), jnp.int32),
            pltpu.VMEM((n, TILE, FI), F32),
            pltpu.SemaphoreType.DMA((4, n)),
        ],
        compiler_params=pltpu.CompilerParams(collective_id=0, has_side_effects=True, vmem_limit_bytes=limit),
        name="fetch",
    )(requests, features)

    unit, per = units(n)
    body = unit * per
    out, ret, fg, msg = pl.pallas_call(
        functools.partial(local_kernel, n),
        out_shape=(shape(rows, WIDTH), shape(n * TILE, FI), shape(rows, FI), shape(n, body + 8, LANES)),
        in_specs=[vmem] * 8,
        out_specs=(vmem,) * 4,
        scratch_shapes=[
            pltpu.VMEM((n * TILE, WIDTH), BF16),
            pltpu.VMEM((n * TILE, WIDTH), BF16),
            pltpu.VMEM((n * TILE, WIDTH), BF16),
            pltpu.VMEM((DEG, rows, WIDTH), F32),
            pltpu.VMEM((DEG * rows, WIDTH), BF16),
            pltpu.VMEM((DEG * rows, WIDTH), BF16),
            pltpu.VMEM((2 * FI, WIDTH), F32),
        ],
        compiler_params=pltpu.CompilerParams(vmem_limit_bytes=limit),
        name="local",
    )(fetched, features, w_left, w_right, attention.reshape(1, WIDTH), src_slot, edge_mask, g_out)

    feature_gradient, grad_left, grad_right, grad_att = pl.pallas_call(
        functools.partial(return_kernel, n),
        out_shape=(shape(rows, FI), shape(FI, WIDTH), shape(FI, WIDTH), shape(HEADS, HD)),
        in_specs=[vmem] * 4,
        out_specs=(vmem,) * 4,
        scratch_shapes=[
            pltpu.VMEM((n, TILE, FI), F32),
            pltpu.VMEM((n, body + 8, LANES), F32),
            pltpu.VMEM((body, LANES), F32),
            pltpu.VMEM((n, body, LANES), F32),
            pltpu.SemaphoreType.DMA((6, n)),
        ],
        compiler_params=pltpu.CompilerParams(collective_id=1, has_side_effects=True, vmem_limit_bytes=limit),
        name="give_back",
    )(ret.reshape(n, TILE, FI), fg, msg, asked)
    return (out, feature_gradient, grad_left, grad_right, grad_att)


def solution(mesh):
    rowwise = P(("group", "row"), None)
    in_specs = (rowwise, P(), P(), P(), rowwise, rowwise, rowwise, rowwise)
    out_specs = (rowwise, rowwise, P("group", None), P("group", None), P("group", None))
    return jax.shard_map(
        on_device, mesh=mesh, in_specs=in_specs, out_specs=out_specs, check_vma=False
    )
```

time: 289 us -> 73.2 us (0.25)
  waiting for transfers between devices: 92.3 us -> 0 us
  Pallas kernels: 0 us -> 64.6 us
  other arithmetic: 58.3 us -> 0 us
  local copies, waits for them, and re-layouts: 62.4 us -> 6.42 us
  blocking collectives: 29.8 us -> 0 us
  starting transfers between devices: 18.1 us -> 0 us
  between operations: 14.3 us -> 0.73 us
  matrix products: 12.2 us -> 0 us
    psum x1 -> x0, waiting for transfers between devices: 89.9 us -> none  [on_device(): lax.psum((left_part, right_part, d_att), 'row')]
    pallas_call x0 -> x3, Pallas kernels: none -> 64.6 us  [the longest x1 32.3 us: on_device(): pl.pallas_call(functools.partial(return_kernel, n), out_shape=(shape(rows...]
    psum x1 -> x0, blocking collectives: 29.8 us -> none  [on_device(): lax.psum((left_part, right_part, d_att), 'row')]
    mul x5 -> x0, local copies, waits for them, and re-layouts: 21.3 us -> none  [the longest x3 13.4 us: attend(): inner = dscore[..., None] * attention[None, None] * slope]
    all_to_all x3 -> x0, starting transfers between devices: 18.1 us -> none  [the longest x1 7.35 us: on_device(): lax.all_to_all(requests, 'row', split_axis=1, concat_axis=1, tiled=True)]
    scatter-add x1 -> x0, other arithmetic: 16 us -> none  [step(): d_left_buf = d_left_buf.at[src_b.reshape(-1)].add(d_l.reshape(-1, width))]
    dot_general x3 -> x0, other arithmetic: 15.4 us -> none  [the longest x1 6.81 us: attend(): score = jnp.einsum('behc,hc->beh', u, attention, precision=HIGH_PRECISION)]
    dot_general x8 -> x0, matrix products: 12.2 us -> none  [the longest x4 5.8 us: matmul(): jnp.dot(first, second, precision=HIGH_PRECISION, preferred_element_type=j...]
  transfers between devices with their start and end apart: 4 -> 0, of which waited for: 2 -> 0; matrix products, arithmetic and copies ran while one was open for 16% -> 0% of each run, Pallas kernels for 0% -> 0%
where the time goes in v1:
time: 73.2 us; the launch traced here: 71.8 us
  Pallas kernels  64.6 us (88%)
  local copies, waits for them, and re-layouts  6.42 us (9%)
    pallas_call x1, Pallas kernels, on_device(): pl.pallas_call(functools.partial(return_kernel, n), out_shape=(shape(rows...  32.3 us
    pallas_call x1, Pallas kernels, on_device(): pl.pallas_call(functools.partial(fetch_kernel, n), out_shape=(shape(n * T...  17.1 us
    pallas_call x1, Pallas kernels, on_device(): pl.pallas_call(functools.partial(local_kernel, n), out_shape=(shape(rows,...  15.3 us
    unnamed x18, local copies, waits for them, and re-layouts  5.65 us

profile of v1, /device:TPU:1, one launch (start us, length us, event | category | flops | bytes accessed | tf_op | source)
XLA Modules:
  0.0 71.8 jit_solution(6090065240669611942)
XLA Ops:
  0.6 0.0 copy-start.5
  0.6 0.0 copy-start.4
  0.7 0.8 %reshape.16.att_ref = f32[1,512]{1,0:T(1,128)S(1)} reshape(f32[8,64]{1,0:T(8,128)} %param.11) | data formatting | bytes 4096 | tf_op jit(solution)/shard_map/reshape | solution.py:364
  1.4 0.0 copy-start.1
  1.4 0.0 copy-start.2
  1.4 0.9 %copy.13.slot_ref = s32[256,8]{1,0:T(8,128)S(1)} copy(s32[256,8]{0,1:T(8,128)} %param.13) | data formatting | bytes 16384 | tf_op args[5]
  2.3 0.0 copy-done.5
  2.3 0.1 copy.14.mask_ref
  2.4 0.0 copy-done.4
  2.5 0.0 copy-done.1
  2.5 17.1 %fetch.1 = (f32[512,128]{1,0:T(8,128)S(1)}, s32[16,8,128]{2,1,0:T(8,128)S(1)}) custom-call(s32[1,16]{1,0:T(1,128)S(1)} %copy-done.4, f32[256,128]{1,0:T(8,128)S(1)} %copy-done.1), custom_call_target="tpu_custom_call" | custom-call | tf_op jit(solution)/shard_map/fetch/pallas_call | solution.py:330
  19.6 0.0 copy-done.2
  19.6 0.0 copy-start
  19.6 1.0 %copy-done = f32[256,512]{1,0:T(8,128)S(1)} copy-done((f32[256,512]{1,0:T(8,128)S(1)}, f32[256,512]{1,0:T(8,128)}, u32[]{:S(2)}) %copy-start) | copy-done | bytes 524312
  20.6 0.0 copy-start.3
  20.6 0.9 %copy-done.3 = f32[128,512]{1,0:T(8,128)S(1)} copy-done((f32[128,512]{1,0:T(8,128)S(1)}, f32[128,512]{1,0:T(8,128)}, u32[]{:S(2)}) %copy-start.3) | copy-done | bytes 262168
  21.6 15.3 %local.1 = (f32[256,512]{1,0:T(8,128)}, f32[512,128]{1,0:T(8,128)S(1)}, f32[256,128]{1,0:T(8,128)S(1)}, f32[16,72,128]{2,1,0:T(8,128)S(1)}) custom-call(f32[512,128]{1,0:T(8,128)S(1)} %get-tuple-element.15.fetched_ref, f32[256,128]{1,0:T(8,128)S(1)} %copy-done.1, f32[128,512]{1,0:T(8,128)S(1)} %copy-done.2, f32[128,512]{1,0:T(8,128)S(1)} %copy-done.3, ...), custom_call_target="tpu_custom_call" | custom-call | tf_op jit(solution)/shard_map/local/pallas_call | solution.py:348
  36.8 32.3 %give_back.1 = (f32[256,128]{1,0:T(8,128)S(1)}, f32[128,512]{1,0:T(8,128)S(1)}, f32[128,512]{1,0:T(8,128)S(1)}, f32[8,64]{1,0:T(8,128)S(1)}) custom-call(f32[16,32,128]{2,1,0:T(8,128)S(1)} %bitcast.1, f32[256,128]{1,0:T(8,128)S(1)} %get-tuple-element.18.fg_ref, f32[16,72,128]{2,1,0:T(8,128)S(1)} %get-tuple-element.19.msg_ref, ...), custom_call_target="tpu_custom_call" | custom-call | tf_op jit(solution)/shard_map/give_back/pallas_call | solution.py:366
  69.1 0.7 copy.19
  69.8 0.7 copy.20
  70.5 0.7 copy.21
  71.2 0.6 copy.22
Async XLA Ops:
  0.6 1.7 %copy-start.5 = (s32[256,8]{0,1:T(8,128)S(1)}, s32[256,8]{0,1:T(8,128)}, u32[]{:S(2)}) copy-start(s32[256,8]{0,1:T(8,128)} %param.14) | copy-start | bytes 24580
  0.6 1.8 %copy-start.4 = (s32[1,16]{1,0:T(1,128)S(1)}, s32[1,16]{1,0:T(1,128)}, u32[]{:S(2)}) copy-start(s32[1,16]{1,0:T(1,128)} %req_ref.1) | copy-start | bytes 196
  1.4 1.0 %copy-start.1 = (f32[256,128]{1,0:T(8,128)S(1)}, f32[256,128]{1,0:T(8,128)}, u32[]{:S(2)}) copy-start(f32[256,128]{1,0:T(8,128)} %feat_ref.3) | copy-start | bytes 393220
  1.4 18.1 %copy-start.2 = (f32[128,512]{1,0:T(8,128)S(1)}, f32[128,512]{1,0:T(8,128)}, u32[]{:S(2)}) copy-start(f32[128,512]{1,0:T(8,128)} %wl_ref.1) | copy-start | bytes 786436
  19.6 1.0 %copy-start = (f32[256,512]{1,0:T(8,128)S(1)}, f32[256,512]{1,0:T(8,128)}, u32[]{:S(2)}) copy-start(f32[256,512]{1,0:T(8,128)} %g_ref.1) | copy-start | bytes 1572868
  20.6 0.9 %copy-start.3 = (f32[128,512]{1,0:T(8,128)S(1)}, f32[128,512]{1,0:T(8,128)}, u32[]{:S(2)}) copy-start(f32[128,512]{1,0:T(8,128)} %wr_ref.1) | copy-start | bytes 786436

commit v2 on v1

--- a/solution.py
+++ b/solution.py
@@ -101,7 +101,7 @@
 
 
 def local_kernel(n, fetched_ref, feat_ref, wl_ref, wr_ref, att_ref, slot_ref, mask_ref, g_ref,
-                 out_ref, ret_ref, fg_ref, msg_ref, hi_ref, mid_ref, lo_ref, le_ref, dhi_ref, dlo_ref, wg_ref):
+                 out_ref, ret_ref, fg_ref, msg_ref, tail_ref, hi_ref, mid_ref, lo_ref, le_ref, dhi_ref, dlo_ref, wg_ref):
     rows = feat_ref.shape[0]
     slots_all = fetched_ref.shape[0]
     chunks = slots_all // CHUNK
@@ -114,9 +114,10 @@
             at = pl.ds(pl.multiple_of(c * CHUNK, CHUNK), CHUNK)
             hi_ref[at], mid_ref[at], lo_ref[at] = split3(dot(fetched_ref[at], wl_ref[...], precision=HIGHEST))
     right = dot(feat_ref[...], wr_ref[...], precision=HIGHEST)
-    att = att_ref[...]
+    att = jnp.concatenate([att_ref[h:h + 1, :] for h in range(HEADS)], axis=1)
     g = g_ref[...]
-    slot = slot_ref[...]
+    slot_t = slot_ref[...]
+    slot = slot_t.T
 
     row_head = lax.broadcasted_iota(jnp.int32, (WIDTH, LANES), 0) // HD
     col = lax.broadcasted_iota(jnp.int32, (WIDTH, LANES), 1)
@@ -150,7 +151,7 @@
 
     spread = (lax.broadcasted_iota(jnp.int32, (DEG, LANES), 0)
               == ((lax.broadcasted_iota(jnp.int32, (DEG, LANES), 1) >> 3) & 7)).astype(F32)
-    alive = dot((mask_ref[...] > 0).astype(F32), spread) > 0.5
+    alive = dot((mask_ref[...].T > 0).astype(F32), spread) > 0.5
 
     def over_edges(x, op):
         for shift in (8, 16, 32):
@@ -192,7 +193,6 @@
         dhi_ref[e * rows:(e + 1) * rows], dlo_ref[e * rows:(e + 1) * rows] = split(prob_w * g + inner)
     out_ref[...] = out
 
-    slot_t = slot.T
     slot_row = lax.broadcasted_iota(jnp.int32, (CHUNK, rows), 0)
 
     def scatter(c):
@@ -225,8 +225,7 @@
             wg_ref[rb * unit:(rb + 1) * unit, lb * LANES:(lb + 1) * LANES])
     att_row = jnp.sum(d_att, axis=0, keepdims=True)
     tail = jnp.concatenate([att_row[:, b * LANES:(b + 1) * LANES] for b in range(4)] + [jnp.zeros((4, LANES), F32)], axis=0)
-    for p in range(n):
-        msg_ref[p, per * unit:] = tail
+    tail_ref[...] = tail
 
 
 def units(n):
@@ -234,55 +233,114 @@
     return unit, (2 * FI // unit) * 4 // n
 
 
-def return_kernel(n, ret_ref, fg_ref, msg_ref, asked_ref, fgo_ref, gl_ref, gr_ref, ga_ref,
-                  ret_in, msg_in, sum_out, sum_in, sems):
+def levels(n):
+    mid = 1
+    while mid * mid * 4 <= n // 2:
+        mid *= 2
+    return n // 2 // mid, mid
+
+
+def return_kernel(n, ret_ref, fg_ref, msg_ref, att_ref, asked_ref, fgo_ref, gl_ref, gr_ref, ga_ref,
+                  ret_in, half_in, half, mid_in, part, outer_in, gathered, att_core, att_mid, att_outer,
+                  ret_sems, sems, att_sems):
     me = lax.axis_index("row")
+    outer, mid = levels(n)
+    plane = mid * outer
+    o, m, c = me // (2 * mid), lax.rem(me // 2, mid), lax.rem(me, 2)
     unit, per = units(n)
-    body = unit * per
     barrier = pltpu.get_barrier_semaphore()
 
-    def remote(src, dst, lane, k):
+    def remote(src, dst, peer, sem, slot):
         return pltpu.make_async_remote_copy(
-            src_ref=src, dst_ref=dst, send_sem=sems.at[2 * lane, k], recv_sem=sems.at[2 * lane + 1, k],
-            device_id={"row": lax.rem(me + k, n)}, device_id_type=MESH)
-
-    def send_msg(k):
-        return remote(msg_ref.at[lax.rem(me + k, n)], msg_in.at[me], 0, k)
+            src_ref=src, dst_ref=dst, send_sem=sem.at[0, slot], recv_sem=sem.at[1, slot],
+            device_id={"row": peer}, device_id_type=MESH)
 
     def send_ret(k):
-        return remote(ret_ref.at[lax.rem(me + k, n)], ret_in.at[me], 1, k)
-
-    def send_sum(k):
-        return remote(sum_out, sum_in.at[me], 2, k)
+        peer = lax.rem(me + k, n)
+        return remote(ret_ref.at[peer], ret_in.at[me], peer, ret_sems, k)
+
+    def mid_peer(k):
+        at = lax.rem(m + k, mid)
+        return at, (o * mid + at) * 2 + c
+
+    def outer_peer(k):
+        at = lax.rem(o + k, outer)
+        return at, (at * mid + m) * 2 + c
+
+    partner = me + 1 - 2 * c
+    first, second, third, fourth = 1, mid, mid + outer, mid + 2 * outer
+    mine = pl.ds(c * plane, plane)
+    block = pl.ds(c * plane + m * outer, outer)
+    spot = c * plane + m * outer + o
 
     greet(n, me, barrier)
 
-    @pl.loop(1, n)
-    def _(k):
-        send_msg(k).start()
+    to_core = [
+        remote(att_ref, att_core, partner, att_sems, 0),
+        remote(msg_ref.at[pl.ds((1 - c) * plane, plane)], half_in, partner, sems, 0),
+    ]
+    for copy in to_core:
+        copy.start()
 
     @pl.loop(1, n)
     def _(k):
         send_ret(k).start()
 
-    msg_in[me] = msg_ref[me]
     ret_in[me] = ret_ref[me]
-
-    @pl.loop(1, n)
-    def _(k):
-        send_msg(k).wait_recv()
-
-    total = lax.fori_loop(1, n, lambda p, acc: acc + msg_in[p], msg_in[0])
-    sum_out[...] = total[:body]
-
-    @pl.loop(1, n)
-    def _(k):
-        send_sum(k).start()
-
-    sum_in[me] = total[:body]
+    for copy in to_core:
+        copy.wait_recv()
+    att_mid[m] = att_ref[...] + att_core[...]
+    half[...] = msg_ref[mine] + half_in[...]
+
+    to_mid = []
+    for k in range(1, mid):
+        at, peer = mid_peer(k)
+        to_mid.append(remote(att_mid.at[m], att_mid.at[m], peer, att_sems, first + k - 1))
+        to_mid.append(remote(half.at[pl.ds(at * outer, outer)], mid_in.at[m], peer, sems, first + k - 1))
+    for copy in to_mid:
+        copy.start()
+    for copy in to_mid:
+        copy.wait_recv()
+    total = half[pl.ds(m * outer, outer)]
+    for k in range(1, mid):
+        total = total + mid_in[lax.rem(m + k, mid)]
+    part[...] = total
+    att = att_mid[0]
+    for k in range(1, mid):
+        att = att + att_mid[k]
+    att_outer[o] = att
+
+    to_outer = []
+    for k in range(1, outer):
+        at, peer = outer_peer(k)
+        to_outer.append(remote(att_outer.at[o], att_outer.at[o], peer, att_sems, second + k - 1))
+        to_outer.append(remote(part.at[at], outer_in.at[o], peer, sems, second + k - 1))
+    for copy in to_outer:
+        copy.start()
+    for copy in to_outer:
+        copy.wait_recv()
+    total = part[o]
+    for k in range(1, outer):
+        total = total + outer_in[lax.rem(o + k, outer)]
+    gathered[spot] = total
+
+    back_outer = [remote(gathered.at[spot], gathered.at[spot], outer_peer(k)[1], sems, third + k - 1)
+                  for k in range(1, outer)]
+    for copy in back_outer:
+        copy.start()
+    att = att_outer[0]
+    for k in range(1, outer):
+        att = att + att_outer[k]
     for b in range(4):
-        ga_ref[2 * b:2 * b + 1] = total[body + b:body + b + 1, :HD]
-        ga_ref[2 * b + 1:2 * b + 2] = total[body + b:body + b + 1, HD:]
+        ga_ref[2 * b:2 * b + 1] = att[b:b + 1, :HD]
+        ga_ref[2 * b + 1:2 * b + 2] = att[b:b + 1, HD:]
+    for copy in back_outer:
+        copy.wait_recv()
+
+    back_mid = [remote(gathered.at[block], gathered.at[block], mid_peer(k)[1], sems, fourth + k - 1)
+                for k in range(1, mid)]
+    for copy in back_mid:
+        copy.start()
 
     @pl.loop(1, n)
     def _(k):
@@ -300,21 +358,24 @@
     for t in range(tiles):
         fgo_ref[t * TILE:(t + 1) * TILE] = done[t].reshape(TILE, FI)
 
-    @pl.loop(1, n)
-    def _(k):
-        send_sum(k).wait_recv()
+    for copy in back_mid:
+        copy.wait_recv()
+    back_core = remote(gathered.at[mine], gathered.at[mine], partner, sems, fourth + mid - 1)
+    back_core.start()
+    back_core.wait_recv()
 
     for u in range(n * per):
         rb, lb = u // 4, u % 4
         ref, base = (gl_ref, 0) if rb * unit < FI else (gr_ref, FI)
         ref[rb * unit - base:(rb + 1) * unit - base, lb * LANES:(lb + 1) * LANES] = (
-            sum_in[u // per, (u % per) * unit:(u % per + 1) * unit])
-
-    @pl.loop(1, n)
-    def _(k):
-        send_msg(k).wait_send()
+            gathered[u // per, (u % per) * unit:(u % per + 1) * unit])
+
+    for copy in to_core + to_mid + to_outer + back_outer + back_mid + [back_core]:
+        copy.wait_send()
+
+    @pl.loop(1, n)
+    def _(k):
         send_ret(k).wait_send()
-        send_sum(k).wait_send()
 
 
 def on_device(features, w_left, w_right, attention, requests, src_slot, edge_mask, g_out):
@@ -345,11 +406,12 @@
 
     unit, per = units(n)
     body = unit * per
-    out, ret, fg, msg = pl.pallas_call(
+    outer, mid = levels(n)
+    out, ret, fg, msg, tail = pl.pallas_call(
         functools.partial(local_kernel, n),
-        out_shape=(shape(rows, WIDTH), shape(n * TILE, FI), shape(rows, FI), shape(n, body + 8, LANES)),
+        out_shape=(shape(rows, WIDTH), shape(n * TILE, FI), shape(rows, FI), shape(n, body, LANES), shape(8, LANES)),
         in_specs=[vmem] * 8,
-        out_specs=(vmem,) * 4,
+        out_specs=(vmem,) * 5,
         scratch_shapes=[
             pltpu.VMEM((n * TILE, WIDTH), BF16),
             pltpu.VMEM((n * TILE, WIDTH), BF16),
@@ -361,23 +423,31 @@
         ],
         compiler_params=pltpu.CompilerParams(vmem_limit_bytes=limit),
         name="local",
-    )(fetched, features, w_left, w_right, attention.reshape(1, WIDTH), src_slot, edge_mask, g_out)
+    )(fetched, features, w_left, w_right, attention, src_slot.T, edge_mask.T, g_out)
 
     feature_gradient, grad_left, grad_right, grad_att = pl.pallas_call(
         functools.partial(return_kernel, n),
         out_shape=(shape(rows, FI), shape(FI, WIDTH), shape(FI, WIDTH), shape(HEADS, HD)),
-        in_specs=[vmem] * 4,
+        in_specs=[vmem] * 5,
         out_specs=(vmem,) * 4,
         scratch_shapes=[
             pltpu.VMEM((n, TILE, FI), F32),
-            pltpu.VMEM((n, body + 8, LANES), F32),
-            pltpu.VMEM((body, LANES), F32),
+            pltpu.VMEM((outer * mid, body, LANES), F32),
+            pltpu.VMEM((outer * mid, body, LANES), F32),
+            pltpu.VMEM((mid, outer, body, LANES), F32),
+            pltpu.VMEM((outer, body, LANES), F32),
+            pltpu.VMEM((outer, body, LANES), F32),
             pltpu.VMEM((n, body, LANES), F32),
-            pltpu.SemaphoreType.DMA((6, n)),
+            pltpu.VMEM((8, LANES), F32),
+            pltpu.VMEM((mid, 8, LANES), F32),
+            pltpu.VMEM((outer, 8, LANES), F32),
+            pltpu.SemaphoreType.DMA((2, n)),
+            pltpu.SemaphoreType.DMA((2, 2 * (outer + mid))),
+            pltpu.SemaphoreType.DMA((2, outer + mid)),
         ],
         compiler_params=pltpu.CompilerParams(collective_id=1, has_side_effects=True, vmem_limit_bytes=limit),
         name="give_back",
-    )(ret.reshape(n, TILE, FI), fg, msg, asked)
+    )(ret.reshape(n, TILE, FI), fg, msg, tail, asked)
     return (out, feature_gradient, grad_left, grad_right, grad_att)
 
 

time: 73.2 us -> 68.6 us (0.937); the launches traced: 71.8 us -> 68.2 us
  Pallas kernels: 64.6 us -> 59 us
  local copies, waits for them, and re-layouts: 6.42 us -> 8.54 us
    pallas_call x1, Pallas kernels: 32.3 us -> 26.5 us  [on_device(): pl.pallas_call(functools.partial(return_kernel, n), out_shape=(shape(rows...]
    unnamed x18 -> x22, local copies, waits for them, and re-layouts: 5.65 us -> 8.54 us
    reshape x1 -> x0, local copies, waits for them, and re-layouts: 0.77 us -> none  [on_device(): attention.reshape(1, WIDTH)]
where the time goes in v2:
time: 68.6 us; the launch traced here: 68.2 us
  Pallas kernels  59 us (86%)
  local copies, waits for them, and re-layouts  8.54 us (12%)
  between operations  0.7 us (1%)
    pallas_call x1, Pallas kernels, on_device(): pl.pallas_call(functools.partial(return_kernel, n), out_shape=(shape(rows...  26.5 us
    pallas_call x1, Pallas kernels, on_device(): pl.pallas_call(functools.partial(fetch_kernel, n), out_shape=(shape(n * T...  17.1 us
    pallas_call x1, Pallas kernels, on_device(): pl.pallas_call(functools.partial(local_kernel, n), out_shape=(shape(rows,...  15.4 us
    unnamed x22, local copies, waits for them, and re-layouts  8.54 us

profile of v2, /device:TPU:1, one launch (start us, length us, event | category | flops | bytes accessed | tf_op | source)
XLA Modules:
  0.0 68.2 jit_solution(1409956954910882353)
XLA Ops:
  0.6 0.0 copy-start.8
  0.6 0.6 copy-done.8
  1.3 0.0 copy-start
  1.3 0.9 %copy-done = f32[256,128]{1,0:T(8,128)S(1)} copy-done((f32[256,128]{1,0:T(8,128)S(1)}, f32[256,128]{1,0:T(8,128)}, u32[]{:S(2)}) %copy-start) | copy-done | bytes 131096
  2.2 0.0 copy-start.1
  2.2 0.0 copy-start.7
  2.2 17.1 %fetch.1 = (f32[512,128]{1,0:T(8,128)S(1)}, s32[16,8,128]{2,1,0:T(8,128)S(1)}) custom-call(s32[1,16]{1,0:T(1,128)S(1)} %copy-done.8, f32[256,128]{1,0:T(8,128)S(1)} %copy-done), custom_call_target="tpu_custom_call" | custom-call | tf_op jit(solution)/shard_map/fetch/pallas_call | solution.py:391
  19.3 0.0 copy-done.1
  19.3 0.0 copy-done.7
  19.3 0.0 copy-start.2
  19.3 1.0 %copy-done.2 = f32[256,512]{1,0:T(8,128)S(1)} copy-done((f32[256,512]{1,0:T(8,128)S(1)}, f32[256,512]{1,0:T(8,128)}, u32[]{:S(2)}) %copy-start.2) | copy-done | bytes 524312
  20.3 0.0 copy-start.3
  20.3 0.9 %copy-done.3 = f32[128,512]{1,0:T(8,128)S(1)} copy-done((f32[128,512]{1,0:T(8,128)S(1)}, f32[128,512]{1,0:T(8,128)}, u32[]{:S(2)}) %copy-start.3) | copy-done | bytes 262168
  21.3 0.0 copy-start.4
  21.3 0.9 %copy-done.4 = f32[128,512]{1,0:T(8,128)S(1)} copy-done((f32[128,512]{1,0:T(8,128)S(1)}, f32[128,512]{1,0:T(8,128)}, u32[]{:S(2)}) %copy-start.4) | copy-done | bytes 262168
  22.2 0.0 copy-start.5
  22.2 0.7 %copy-done.5 = s32[256,8]{0,1:T(8,128)S(1)} copy-done((s32[256,8]{0,1:T(8,128)S(1)}, s32[256,8]{0,1:T(8,128)}, u32[]{:S(2)}) %copy-start.5) | copy-done | bytes 8216
  22.9 0.0 copy-start.6
  22.9 0.7 %copy-done.6 = s32[256,8]{0,1:T(8,128)S(1)} copy-done((s32[256,8]{0,1:T(8,128)S(1)}, s32[256,8]{0,1:T(8,128)}, u32[]{:S(2)}) %copy-start.6) | copy-done | bytes 8216
  23.6 15.4 %local.1 = (f32[256,512]{1,0:T(8,128)}, f32[512,128]{1,0:T(8,128)S(1)}, f32[256,128]{1,0:T(8,128)S(1)}, f32[16,64,128]{2,1,0:T(8,128)S(1)}, f32[8,128]{1,0:T(8,128)S(1)}) custom-call(f32[512,128]{1,0:T(8,128)S(1)} %get-tuple-element.16.fetched_ref, f32[256,128]{1,0:T(8,128)S(1)} %copy-done.1, f32[128,512]{1,0:T(8,128)S(1)} %copy-done.3, ...), custom_call_target="tpu_custom_call" | custom-call | tf_op jit(solution)/shard_map/local/pallas_call | solution.py:410
  39.0 26.5 %give_back.1 = (f32[256,128]{1,0:T(8,128)S(1)}, f32[128,512]{1,0:T(8,128)S(1)}, f32[128,512]{1,0:T(8,128)S(1)}, f32[8,64]{1,0:T(8,128)S(1)}) custom-call(f32[16,32,128]{2,1,0:T(8,128)S(1)} %bitcast.3, f32[256,128]{1,0:T(8,128)S(1)} %get-tuple-element.19.fg_ref, f32[16,64,128]{2,1,0:T(8,128)S(1)} %get-tuple-element.20.msg_ref, ...), custom_call_target="tpu_custom_call" | custom-call | tf_op jit(solution)/shard_map/give_back/pallas_call | solution.py:428
  65.6 0.7 copy.17
  66.2 0.7 %copy.18 = f32[128,512]{1,0:T(8,128)} copy(f32[128,512]{1,0:T(8,128)S(1)} %get-tuple-element.34) | data formatting | bytes 524288
  66.9 0.7 %copy.19 = f32[128,512]{1,0:T(8,128)} copy(f32[128,512]{1,0:T(8,128)S(1)} %get-tuple-element.35) | data formatting | bytes 524288
  67.6 0.6 copy.20
Async XLA Ops:
  0.6 0.7 copy-start.8
  1.3 0.9 %copy-start = (f32[256,128]{1,0:T(8,128)S(1)}, f32[256,128]{1,0:T(8,128)}, u32[]{:S(2)}) copy-start(f32[256,128]{1,0:T(8,128)} %feat_ref.3) | copy-start | bytes 393220
  2.2 17.1 %copy-start.1 = (f32[256,128]{1,0:T(8,128)S(1)}, f32[256,128]{1,0:T(8,128)}, u32[]{:S(2)}) copy-start(f32[256,128]{1,0:T(8,128)} %feat_ref.3) | copy-start | bytes 393220
  2.2 17.1 %copy-start.7 = (f32[8,64]{1,0:T(8,128)S(1)}, f32[8,64]{1,0:T(8,128)}, u32[]{:S(2)}) copy-start(f32[8,64]{1,0:T(8,128)} %att_ref.1) | copy-start | bytes 6148
  19.3 1.0 %copy-start.2 = (f32[256,512]{1,0:T(8,128)S(1)}, f32[256,512]{1,0:T(8,128)}, u32[]{:S(2)}) copy-start(f32[256,512]{1,0:T(8,128)} %g_ref.1) | copy-start | bytes 1572868
  20.3 0.9 %copy-start.3 = (f32[128,512]{1,0:T(8,128)S(1)}, f32[128,512]{1,0:T(8,128)}, u32[]{:S(2)}) copy-start(f32[128,512]{1,0:T(8,128)} %wl_ref.1) | copy-start | bytes 786436
  21.3 0.9 %copy-start.4 = (f32[128,512]{1,0:T(8,128)S(1)}, f32[128,512]{1,0:T(8,128)}, u32[]{:S(2)}) copy-start(f32[128,512]{1,0:T(8,128)} %wr_ref.1) | copy-start | bytes 786436
  22.2 0.7 %copy-start.5 = (s32[256,8]{0,1:T(8,128)S(1)}, s32[256,8]{0,1:T(8,128)}, u32[]{:S(2)}) copy-start(s32[256,8]{0,1:T(8,128)} %param.13) | copy-start | bytes 24580
  22.9 0.7 %copy-start.6 = (s32[256,8]{0,1:T(8,128)S(1)}, s32[256,8]{0,1:T(8,128)}, u32[]{:S(2)}) copy-start(s32[256,8]{0,1:T(8,128)} %param.14) | copy-start | bytes 24580

commit v3 on v2

--- a/solution.py
+++ b/solution.py
@@ -36,6 +36,12 @@
     rest = x - hi.astype(F32)
     mid = rest.astype(BF16)
     return hi, mid, (rest - mid.astype(F32)).astype(BF16)
+
+
+def dot3(a, b, dims=((1,), (0,))):
+    a_hi, a_lo = split(a)
+    b_hi, b_lo = split(b)
+    return dot(a_hi, b_hi, dims) + (dot(a_hi, b_lo, dims) + dot(a_lo, b_hi, dims))
 
 
 def greet(n, me, barrier):
@@ -204,8 +210,8 @@
 
     if chunks == 1:
         d_left = scatter(0)
-        ret_ref[...] = dot(d_left, wl_ref[...], ((1,), (1,)), precision=HIGHEST)
-        wg_ref[0:FI] = dot(fetched_ref[...].T, d_left, precision=HIGHEST)
+        ret_ref[...] = dot3(d_left, wl_ref[...], ((1,), (1,)))
+        wg_ref[0:FI] = dot3(fetched_ref[...].T, d_left)
     else:
         wg_ref[0:FI] = jnp.zeros((FI, WIDTH), F32)
 
@@ -213,10 +219,10 @@
         def _(c):
             at = pl.ds(pl.multiple_of(c * CHUNK, CHUNK), CHUNK)
             d_left = scatter(c)
-            ret_ref[at] = dot(d_left, wl_ref[...], ((1,), (1,)), precision=HIGHEST)
-            wg_ref[0:FI] += dot(fetched_ref[at].T, d_left, precision=HIGHEST)
-    fg_ref[...] = dot(d_right, wr_ref[...], ((1,), (1,)), precision=HIGHEST)
-    wg_ref[FI:2 * FI] = dot(feat_ref[...].T, d_right, precision=HIGHEST)
+            ret_ref[at] = dot3(d_left, wl_ref[...], ((1,), (1,)))
+            wg_ref[0:FI] += dot3(fetched_ref[at].T, d_left)
+    fg_ref[...] = dot3(d_right, wr_ref[...], ((1,), (1,)))
+    wg_ref[FI:2 * FI] = dot3(feat_ref[...].T, d_right)
 
     unit, per = units(n)
     for u in range(n * per):
@@ -242,7 +248,7 @@
 
 def return_kernel(n, ret_ref, fg_ref, msg_ref, att_ref, asked_ref, fgo_ref, gl_ref, gr_ref, ga_ref,
                   ret_in, half_in, half, mid_in, part, outer_in, gathered, att_core, att_mid, att_outer,
-                  ret_sems, sems, att_sems):
+                  ret_sems, sems, att_sems, chunk_sems, core_sems):
     me = lax.axis_index("row")
     outer, mid = levels(n)
     plane = mid * outer
@@ -268,9 +274,8 @@
         return at, (at * mid + m) * 2 + c
 
     partner = me + 1 - 2 * c
-    first, second, third, fourth = 1, mid, mid + outer, mid + 2 * outer
+    first, second, third = 1, mid, mid + outer
     mine = pl.ds(c * plane, plane)
-    block = pl.ds(c * plane + m * outer, outer)
     spot = c * plane + m * outer + o
 
     greet(n, me, barrier)
@@ -294,29 +299,40 @@
 
     to_mid = []
     for k in range(1, mid):
-        at, peer = mid_peer(k)
-        to_mid.append(remote(att_mid.at[m], att_mid.at[m], peer, att_sems, first + k - 1))
-        to_mid.append(remote(half.at[pl.ds(at * outer, outer)], mid_in.at[m], peer, sems, first + k - 1))
+        to_mid.append(remote(att_mid.at[m], att_mid.at[m], mid_peer(k)[1], att_sems, first + k - 1))
+    mid_chunks = []
+    for j in list(range(1, outer)) + [0]:
+        there = lax.rem(o + j, outer)
+        mid_chunks.append((there, [
+            remote(half.at[mid_peer(k)[0] * outer + there], mid_in.at[m, there], mid_peer(k)[1], chunk_sems, (k - 1) * outer + j)
+            for k in range(1, mid)]))
     for copy in to_mid:
         copy.start()
+    for _, copies in mid_chunks:
+        for copy in copies:
+            copy.start()
     for copy in to_mid:
         copy.wait_recv()
-    total = half[pl.ds(m * outer, outer)]
-    for k in range(1, mid):
-        total = total + mid_in[lax.rem(m + k, mid)]
-    part[...] = total
     att = att_mid[0]
     for k in range(1, mid):
         att = att + att_mid[k]
     att_outer[o] = att
 
-    to_outer = []
-    for k in range(1, outer):
-        at, peer = outer_peer(k)
-        to_outer.append(remote(att_outer.at[o], att_outer.at[o], peer, att_sems, second + k - 1))
-        to_outer.append(remote(part.at[at], outer_in.at[o], peer, sems, second + k - 1))
+    to_outer = [remote(att_outer.at[o], att_outer.at[o], outer_peer(k)[1], att_sems, second + k - 1)
+                for k in range(1, outer)]
     for copy in to_outer:
         copy.start()
+    for j, (there, copies) in enumerate(mid_chunks, 1):
+        for copy in copies:
+            copy.wait_recv()
+        total = half[m * outer + there]
+        for k in range(1, mid):
+            total = total + mid_in[lax.rem(m + k, mid), there]
+        part[there] = total
+        if j < outer:
+            copy = remote(part.at[there], outer_in.at[o], outer_peer(j)[1], sems, second + j - 1)
+            copy.start()
+            to_outer.append(copy)
     for copy in to_outer:
         copy.wait_recv()
     total = part[o]
@@ -324,9 +340,22 @@
         total = total + outer_in[lax.rem(o + k, outer)]
     gathered[spot] = total
 
+    def place(km, j):
+        return c * plane + lax.rem(m - km + mid, mid) * outer + lax.rem(o - j + outer, outer)
+
+    def pass_core(km, j):
+        at = gathered.at[place(km, j)]
+        return remote(at, at, partner, core_sems, km * outer + j)
+
+    def pass_mid(k, j):
+        at = gathered.at[place(0, j)]
+        return remote(at, at, mid_peer(k)[1], chunk_sems, (mid - 1) * outer + (k - 1) * outer + j)
+
     back_outer = [remote(gathered.at[spot], gathered.at[spot], outer_peer(k)[1], sems, third + k - 1)
                   for k in range(1, outer)]
-    for copy in back_outer:
+    back_mid = [[pass_mid(k, j) for k in range(1, mid)] for j in range(outer)]
+    back_core = {(km, j): pass_core(km, j) for km in range(mid) for j in range(outer)}
+    for copy in back_outer + back_mid[0] + [back_core[0, 0]]:
         copy.start()
     att = att_outer[0]
     for k in range(1, outer):
@@ -334,13 +363,14 @@
     for b in range(4):
         ga_ref[2 * b:2 * b + 1] = att[b:b + 1, :HD]
         ga_ref[2 * b + 1:2 * b + 2] = att[b:b + 1, HD:]
-    for copy in back_outer:
-        copy.wait_recv()
-
-    back_mid = [remote(gathered.at[block], gathered.at[block], mid_peer(k)[1], sems, fourth + k - 1)
-                for k in range(1, mid)]
-    for copy in back_mid:
-        copy.start()
+    for j in range(1, outer):
+        back_outer[j - 1].wait_recv()
+        for copy in back_mid[j] + [back_core[0, j]]:
+            copy.start()
+    for j in range(outer):
+        for k in range(1, mid):
+            back_mid[j][k - 1].wait_recv()
+            back_core[k, j].start()
 
     @pl.loop(1, n)
     def _(k):
@@ -358,11 +388,8 @@
     for t in range(tiles):
         fgo_ref[t * TILE:(t + 1) * TILE] = done[t].reshape(TILE, FI)
 
-    for copy in back_mid:
+    for copy in back_core.values():
         copy.wait_recv()
-    back_core = remote(gathered.at[mine], gathered.at[mine], partner, sems, fourth + mid - 1)
-    back_core.start()
-    back_core.wait_recv()
 
     for u in range(n * per):
         rb, lb = u // 4, u % 4
@@ -370,7 +397,8 @@
         ref[rb * unit - base:(rb + 1) * unit - base, lb * LANES:(lb + 1) * LANES] = (
             gathered[u // per, (u % per) * unit:(u % per + 1) * unit])
 
-    for copy in to_core + to_mid + to_outer + back_outer + back_mid + [back_core]:
+    passed = [copy for _, copies in mid_chunks for copy in copies] + [copy for copies in back_mid for copy in copies]
+    for copy in to_core + to_mid + to_outer + back_outer + passed + list(back_core.values()):
         copy.wait_send()
 
     @pl.loop(1, n)
@@ -401,6 +429,7 @@
             pltpu.SemaphoreType.DMA((4, n)),
         ],
         compiler_params=pltpu.CompilerParams(collective_id=0, has_side_effects=True, vmem_limit_bytes=limit),
+        cost_estimate=pl.CostEstimate(flops=12 * 10**9, bytes_accessed=48 * 2**20, transcendentals=0),
         name="fetch",
     )(requests, features)
 
@@ -422,6 +451,7 @@
             pltpu.VMEM((2 * FI, WIDTH), F32),
         ],
         compiler_params=pltpu.CompilerParams(vmem_limit_bytes=limit),
+        cost_estimate=pl.CostEstimate(flops=12 * 10**9, bytes_accessed=4 * 2**20, transcendentals=0),
         name="local",
     )(fetched, features, w_left, w_right, attention, src_slot.T, edge_mask.T, g_out)
 
@@ -444,6 +474,8 @@
             pltpu.SemaphoreType.DMA((2, n)),
             pltpu.SemaphoreType.DMA((2, 2 * (outer + mid))),
             pltpu.SemaphoreType.DMA((2, outer + mid)),
+            pltpu.SemaphoreType.DMA((2, 2 * mid * outer)),
+            pltpu.SemaphoreType.DMA((2, mid * outer)),
         ],
         compiler_params=pltpu.CompilerParams(collective_id=1, has_side_effects=True, vmem_limit_bytes=limit),
         name="give_back",

time: 68.6 us -> 61 us (0.89)
  local copies, waits for them, and re-layouts: 8.54 us -> 4.23 us
  Pallas kernels: 59 us -> 55.9 us
    unnamed x22, local copies, waits for them, and re-layouts: 8.54 us -> 4.23 us
    pallas_call x1, Pallas kernels: 26.5 us -> 24.5 us  [on_device(): pl.pallas_call(functools.partial(return_kernel, n), out_shape=(shape(rows...]
    pallas_call x1, Pallas kernels: 15.4 us -> 14.4 us  [on_device(): pl.pallas_call(functools.partial(local_kernel, n), out_shape=(shape(rows,...]
where the time goes in v3:
time: 61 us; the launch traced here: 60.9 us
  Pallas kernels  55.9 us (92%)
  local copies, waits for them, and re-layouts  4.23 us (7%)
  between operations  0.75 us (1%)
    pallas_call x1, Pallas kernels, on_device(): pl.pallas_call(functools.partial(return_kernel, n), out_shape=(shape(rows...  24.5 us
    pallas_call x1, Pallas kernels, on_device(): pl.pallas_call(functools.partial(fetch_kernel, n), out_shape=(shape(n * T...  17.1 us
    pallas_call x1, Pallas kernels, on_device(): pl.pallas_call(functools.partial(local_kernel, n), out_shape=(shape(rows,...  14.4 us
    unnamed x22, local copies, waits for them, and re-layouts  4.23 us

profile of v3, /device:TPU:1, one launch (start us, length us, event | category | flops | bytes accessed | tf_op | source)
XLA Modules:
  0.0 60.9 jit_solution(18299221779095171559)
XLA Ops:
  0.6 0.0 copy-start.8
  0.6 0.6 %copy-done.8 = s32[1,16]{1,0:T(1,128)S(1)} copy-done((s32[1,16]{1,0:T(1,128)S(1)}, s32[1,16]{1,0:T(1,128)}, u32[]{:S(2)}) %copy-start.8) | copy-done | bytes 88
  1.3 0.0 copy-start.3
  1.3 0.9 %copy-done.3 = f32[256,128]{1,0:T(8,128)S(1)} copy-done((f32[256,128]{1,0:T(8,128)S(1)}, f32[256,128]{1,0:T(8,128)}, u32[]{:S(2)}) %copy-start.3) | copy-done | bytes 131096
  2.2 0.0 copy-start
  2.2 0.0 copy-start.1
  2.2 0.0 copy-start.2
  2.2 0.0 copy-start.4
  2.2 0.0 copy-start.5
  2.2 0.0 copy-start.6
  2.2 0.0 copy-start.7
  2.2 17.1 %fetch.1 = (f32[512,128]{1,0:T(8,128)S(1)}, s32[16,8,128]{2,1,0:T(8,128)S(1)}) custom-call(s32[1,16]{1,0:T(1,128)S(1)} %copy-done.8, f32[256,128]{1,0:T(8,128)S(1)} %copy-done.3), custom_call_target="tpu_custom_call" | custom-call | flops 12000000000 | bytes 50331648 | tf_op jit(solution)/shard_map/fetch/pallas_call | solution.py:419
  19.3 0.0 copy-done
  19.3 0.0 copy-done.1
  19.3 0.0 copy-done.2
  19.4 0.0 copy-done.4
  19.4 0.0 copy-done.5
  19.4 0.0 copy-done.6
  19.4 0.0 copy-done.7
  19.4 14.4 %local.1 = (f32[256,512]{1,0:T(8,128)}, f32[512,128]{1,0:T(8,128)S(1)}, f32[256,128]{1,0:T(8,128)S(1)}, f32[16,64,128]{2,1,0:T(8,128)S(1)}, f32[8,128]{1,0:T(8,128)S(1)}) custom-call(f32[512,128]{1,0:T(8,128)S(1)} %get-tuple-element.16.fetched_ref, f32[256,128]{1,0:T(8,128)S(1)} %copy-done.4, f32[128,512]{1,0:T(8,128)S(1)} %copy-done.1, ...), custom_call_target="tpu_custom_call" | custom-call | flops 12000000000 | bytes 4194304 | tf_op jit(solution)/shard_map/local/pallas_call | solution.py:439
  33.8 24.5 %give_back.1 = (f32[256,128]{1,0:T(8,128)S(1)}, f32[128,512]{1,0:T(8,128)S(1)}, f32[128,512]{1,0:T(8,128)S(1)}, f32[8,64]{1,0:T(8,128)S(1)}) custom-call(f32[16,32,128]{2,1,0:T(8,128)S(1)} %bitcast.3, f32[256,128]{1,0:T(8,128)S(1)} %get-tuple-element.19.fg_ref, f32[16,64,128]{2,1,0:T(8,128)S(1)} %get-tuple-element.20.msg_ref, ...), custom_call_target="tpu_custom_call" | custom-call | tf_op jit(solution)/shard_map/give_back/pallas_call | solution.py:458
  58.2 0.7 %copy.17 = f32[256,128]{1,0:T(8,128)} copy(f32[256,128]{1,0:T(8,128)S(1)} %get-tuple-element.33) | data formatting | bytes 262144
  58.9 0.7 %copy.18 = f32[128,512]{1,0:T(8,128)} copy(f32[128,512]{1,0:T(8,128)S(1)} %get-tuple-element.34) | data formatting | bytes 524288
  59.6 0.7 %copy.19 = f32[128,512]{1,0:T(8,128)} copy(f32[128,512]{1,0:T(8,128)S(1)} %get-tuple-element.35) | data formatting | bytes 524288
  60.3 0.6 copy.20
Async XLA Ops:
  0.6 0.7 %copy-start.8 = (s32[1,16]{1,0:T(1,128)S(1)}, s32[1,16]{1,0:T(1,128)}, u32[]{:S(2)}) copy-start(s32[1,16]{1,0:T(1,128)} %req_ref.1) | copy-start | bytes 196
  1.3 0.9 %copy-start.3 = (f32[256,128]{1,0:T(8,128)S(1)}, f32[256,128]{1,0:T(8,128)}, u32[]{:S(2)}) copy-start(f32[256,128]{1,0:T(8,128)} %feat_ref.3) | copy-start | bytes 393220
  2.2 17.1 %copy-start = (f32[256,512]{1,0:T(8,128)S(1)}, f32[256,512]{1,0:T(8,128)}, u32[]{:S(2)}) copy-start(f32[256,512]{1,0:T(8,128)} %g_ref.1) | copy-start | bytes 1572868
  2.2 17.1 %copy-start.1 = (f32[128,512]{1,0:T(8,128)S(1)}, f32[128,512]{1,0:T(8,128)}, u32[]{:S(2)}) copy-start(f32[128,512]{1,0:T(8,128)} %wl_ref.1) | copy-start | bytes 786436
  2.2 17.1 %copy-start.2 = (f32[128,512]{1,0:T(8,128)S(1)}, f32[128,512]{1,0:T(8,128)}, u32[]{:S(2)}) copy-start(f32[128,512]{1,0:T(8,128)} %wr_ref.1) | copy-start | bytes 786436
  2.2 17.2 %copy-start.4 = (f32[256,128]{1,0:T(8,128)S(1)}, f32[256,128]{1,0:T(8,128)}, u32[]{:S(2)}) copy-start(f32[256,128]{1,0:T(8,128)} %feat_ref.3) | copy-start | bytes 393220
  2.2 17.2 %copy-start.5 = (s32[256,8]{0,1:T(8,128)S(1)}, s32[256,8]{0,1:T(8,128)}, u32[]{:S(2)}) copy-start(s32[256,8]{0,1:T(8,128)} %param.13) | copy-start | bytes 24580
  2.2 17.2 %copy-start.6 = (s32[256,8]{0,1:T(8,128)S(1)}, s32[256,8]{0,1:T(8,128)}, u32[]{:S(2)}) copy-start(s32[256,8]{0,1:T(8,128)} %param.14) | copy-start | bytes 24580
  2.2 17.2 %copy-start.7 = (f32[8,64]{1,0:T(8,128)S(1)}, f32[8,64]{1,0:T(8,128)}, u32[]{:S(2)}) copy-start(f32[8,64]{1,0:T(8,128)} %att_ref.1) | copy-start | bytes 6148
